TPU v7x, 512 devices: a whole 4x4x16 slice. The times are simulated.
512 devices in a mesh: chain: 64 (over z, y), rows: 8 (over x, core).
Axes of the slice: x: 4, y: 4, z: 16, core: 2. Of those that a mesh axis runs over, the one named last changes fastest.
Arguments:
- sites: float32 [64, 512, 2, 512], P('chain', 'rows'), as said below
- angles: float32 [64, 2], P('chain'), may hold values from -3.140625 to 3.140625
- sketch: float32 [1024, 512], replicated, may hold values from -0.1875 to 0.1875
Outputs:
- new_sites: float32 [64, 512, 2, 512], P('chain', 'rows')
Inputs may be any that keep to these rules, and one draw needn't show every extreme that they name: `sites`: real site tensors.
All inputs are finite; a program needn't handle non-finite values.
Results may differ from a plain program's by a relative error of at most 0.0003.
Values sent between devices are 32-bit elements; how exact they have to be, the bound alone decides.
A program may use at most 64 MiB of HBM per device.

v0:
```python
import jax
import jax.numpy as jnp
from jax import lax
from jax.sharding import PartitionSpec as P

ITERS = 6


HIGH = lax.Precision.HIGHEST


def from_partner(block, axis, distance):
    count = lax.axis_size(axis)
    route = []
    for low in range(count):
        high = low | 1 << distance
        if high != low and high < count:
            route += [(low, high), (high, low)]
    return lax.ppermute(block, axis, route)


def rotation(angle):
    cosine = jnp.cos(angle)
    sine = jnp.sin(angle)
    return jnp.stack([jnp.stack([cosine, -sine]), jnp.stack([sine, cosine])])


def gate_of(left_angles, right_angles):
    coupling = 0.5 * (left_angles[1] + right_angles[1])
    kick = jnp.kron(rotation(left_angles[0]), rotation(right_angles[0]))
    flip = jnp.kron(
        jnp.array([[0.0, 1.0], [-1.0, 0.0]], jnp.float32),
        jnp.array([[0.0, 1.0], [1.0, 0.0]], jnp.float32),
    )
    mixer = jnp.cos(coupling) * jnp.eye(4, dtype=jnp.float32) + jnp.sin(coupling) * flip
    return jnp.dot(kick, mixer, precision=HIGH)


def refine(own, normed, inverse):
    product = jnp.dot(
        jnp.dot(jnp.dot(own, normed, precision=HIGH), inverse, precision=HIGH),
        inverse,
        precision=HIGH,
    )
    return 1.5 * own - 0.5 * product


def per_device(sites, angles, sketch):
    parity = lax.axis_index("chain") % 2
    is_even = parity == 0
    other_sites, other_angles = from_partner((sites, angles), "chain", 0)
    left = jnp.where(is_even, sites, other_sites)[0]
    right = jnp.where(is_even, other_sites, sites)[0]
    left_angles = jnp.where(is_even, angles, other_angles)[0]
    right_angles = jnp.where(is_even, other_angles, angles)[0]
    local_rows = left.shape[0]
    width = left.shape[2]
    left_mat = left.reshape(2 * local_rows, width)
    right_mat = right.reshape(local_rows, 2 * width)
    theta = jnp.dot(left_mat, lax.all_gather(right_mat, "rows", axis=0, tiled=True), precision=HIGH)
    gate = gate_of(left_angles, right_angles).reshape(2, 2, 2, 2)
    theta = jnp.einsum(
        "pqst,lstr->lpqr", gate, theta.reshape(local_rows, 2, 2, width), precision=HIGH
    )
    theta = theta.reshape(2 * local_rows, 2 * width)
    sketched = jnp.dot(theta, sketch, precision=HIGH)
    gram = lax.psum(jnp.dot(sketched.T, sketched, precision=HIGH), "rows")
    scale = jnp.sqrt(jnp.sum(gram * gram) + 1e-06)
    normed = gram / scale
    inverse = jnp.eye(width, dtype=jnp.float32)
    half_rows = width // 2
    first_row = parity * half_rows
    for step in range(ITERS):
        own = lax.dynamic_slice_in_dim(inverse, first_row, half_rows, 0)
        fresh = refine(own, normed, inverse)
        across = from_partner(fresh, "chain", 0)
        inverse = jnp.where(
            is_even, jnp.concatenate([fresh, across], 0), jnp.concatenate([across, fresh], 0)
        )
    basis = jnp.dot(sketched, inverse, precision=HIGH) * jnp.sqrt(2.0 * width / scale)
    new_left = basis.reshape(local_rows, 2, width)
    new_right = lax.psum_scatter(
        jnp.dot(basis.T, theta, precision=HIGH) / (2.0 * width),
        "rows",
        scatter_dimension=0,
        tiled=True,
    )
    new_right = new_right.reshape(local_rows, 2, width)
    return jnp.where(is_even, new_left, new_right)[None]


def solution(mesh):
    in_specs = (P("chain", "rows", None, None), P("chain", None), P())
    out_specs = P("chain", "rows", None, None)
    return jax.shard_map(
        per_device, mesh=mesh, in_specs=in_specs, out_specs=out_specs, check_vma=False
    )
```

profile of v0, /device:TPU:1, one launch (start us, length us, event | category | flops | bytes accessed | tf_op | source)
XLA Modules:
  0.0 310.3 jit_solution(10069717177624012471)
XLA Ops:
  6.5 4.2 %collective-permute-start = (f32[1,64,2,512]{3,2,1,0:T(2,128)}, f32[1,64,2,512]{3,2,1,0:T(2,128)S(1)}, u32[]{:S(2)}, u32[]{:S(2)}) collective-permute-start(f32[1,64,2,512]{3,2,1,0:T(2,128)} %param.5), channel_id=1, source_target_pairs={{0,8},{8,0},{16,24},{24,16},{32,40},{40,32},{48,56},{56,48},{64,72... | collective-permute-start | bytes 786440 | tf_op jit(solution)/shard_map/ppermute | solution.py:19
  10.7 3.9 %collective-permute-done = f32[1,64,2,512]{3,2,1,0:T(2,128)S(1)} collective-permute-done((f32[1,64,2,512]{3,2,1,0:T(2,128)}, f32[1,64,2,512]{3,2,1,0:T(2,128)S(1)}, u32[]{:S(2)}, u32[]{:S(2)}) %collective-permute-start) | collective-permute-done | bytes 262176 | tf_op jit(solution)/shard_map/ppermute | solution.py:19
  14.7 1.1 select_bitcast_fusion
  15.8 0.8 copy.15
  16.6 3.4 %collective-permute-start.1 = (f32[1,2]{1,0:T(1,128)}, f32[1,2]{1,0:T(1,128)S(1)}, u32[]{:S(2)}, u32[]{:S(2)}) collective-permute-start(f32[1,2]{1,0:T(1,128)} %param.6), channel_id=1, source_target_pairs={{0,8},{8,0},{16,24},{24,16},{32,40},{40,32},{48,56},{56,48},{64,72... | collective-permute-start | bytes 32 | tf_op jit(solution)/shard_map/ppermute | solution.py:19
  20.0 1.4 collective-permute-done.1
  21.4 0.7 broadcast_select_fusion.2
  22.1 0.7 fusion.39
  27.0 0.1 mul.122
  27.2 0.1 mul.125
  27.3 0.8 multiply_multiply_fusion
  28.1 0.1 mul.136
  28.2 0.1 copy.6
  28.3 0.2 convolution_bitcast_fusion
  28.5 28.9 %all-gather.2.cloned.1.call-done = f32[512,1024]{1,0:T(8,128)} async-done(((f32[64,1024]{1,0:T(8,128)}), f32[512,1024]{1,0:T(8,128)}) %all-gather.2.cloned.1.call-update) | async-done | bytes 2097168 | tf_op jit(solution)/shard_map/all_gather | solution.py:60
  57.4 4.0 %reshape.84 = f32[2,512,512,1]{1,0,2,3:T(2,128)} reshape(f32[1024,512]{0,1:T(8,128)} %bitcast.82) | data formatting | bytes 4194304 | tf_op jit(solution)/shard_map/dot_general | solution.py:60
  61.4 3.1 %fusion.2 = f32[64,2,2,512,1]{3,0,2,1,4:T(8,128)S(1)} fusion(f32[2,512,512,1]{1,0,2,3:T(2,128)} %reshape.84, f32[64,2,512,1]{2,1,0,3:T(2,128)S(1)} %get-tuple-element.5), kind=kOutput, calls=%fused_computation.8 | convolution fusion | flops 805306368 | bytes 2883584 | tf_op jit(solution)/shard_map/dot_general | solution.py:60
  64.5 2.2 fusion.12
  66.7 0.1 copy.16
  66.9 1.3 fusion.41
  68.2 2.0 fusion.42
  70.4 76.2 %all-reduce.2.cloned.1.call-done = f32[512,512]{1,0:T(8,128)} async-done(((f32[512,512]{1,0:T(8,128)}), f32[512,512]{1,0:T(8,128)}) %all-reduce.2.cloned.1.call-update) | async-done | bytes 1048592 | tf_op jit(solution)/shard_map/psum | solution.py:67
  146.6 2.1 multiply_reduce_fusion
  149.4 1.9 fusion.25
  151.3 0.6 fusion.11
  151.9 0.6 fusion.5
  152.5 2.8 collective-permute-start.2
  155.3 10.2 %collective-permute-done.2 = f32[256,512]{1,0:T(8,128)S(1)} collective-permute-done((f32[256,512]{1,0:T(8,128)S(1)}, f32[256,512]{1,0:T(8,128)S(1)}, u32[]{:S(2)}, u32[]{:S(2)}) %collective-permute-start.2) | collective-permute-done | bytes 524320 | tf_op jit(solution)/shard_map/ppermute | solution.py:19
  165.6 0.1 maximum_select_fusion
  165.7 1.1 fusion.23
  166.8 1.1 fusion.43
  167.9 1.1 multiply_subtract_fusion.4
  168.9 2.2 collective-permute-start.3
  171.1 9.9 %collective-permute-done.3 = f32[256,512]{1,0:T(8,128)S(1)} collective-permute-done((f32[256,512]{1,0:T(8,128)S(1)}, f32[256,512]{1,0:T(8,128)S(1)}, u32[]{:S(2)}, u32[]{:S(2)}) %collective-permute-start.3) | collective-permute-done | bytes 524320 | tf_op jit(solution)/shard_map/ppermute | solution.py:19
  181.1 0.1 maximum_select_fusion.1
  181.2 1.1 fusion.21
  182.3 1.1 fusion.44
  183.4 1.1 multiply_subtract_fusion.3
  184.4 1.9 collective-permute-start.4
  186.3 9.3 %collective-permute-done.4 = f32[256,512]{1,0:T(8,128)S(1)} collective-permute-done((f32[256,512]{1,0:T(8,128)S(1)}, f32[256,512]{1,0:T(8,128)S(1)}, u32[]{:S(2)}, u32[]{:S(2)}) %collective-permute-start.4) | collective-permute-done | bytes 524320 | tf_op jit(solution)/shard_map/ppermute | solution.py:19
  195.6 0.1 maximum_select_fusion.2
  195.8 1.1 fusion.19
  196.9 1.1 fusion.45
  197.9 1.1 multiply_subtract_fusion.2
  199.0 2.1 collective-permute-start.5
  201.1 8.2 %collective-permute-done.5 = f32[256,512]{1,0:T(8,128)S(1)} collective-permute-done((f32[256,512]{1,0:T(8,128)S(1)}, f32[256,512]{1,0:T(8,128)S(1)}, u32[]{:S(2)}, u32[]{:S(2)}) %collective-permute-start.5) | collective-permute-done | bytes 524320 | tf_op jit(solution)/shard_map/ppermute | solution.py:19
  209.3 0.1 maximum_select_fusion.3
  209.4 1.1 fusion.17
  210.5 1.1 fusion.46
  211.6 1.1 multiply_subtract_fusion.1
  212.6 1.9 collective-permute-start.6
  214.6 8.0 %collective-permute-done.6 = f32[256,512]{1,0:T(8,128)S(1)} collective-permute-done((f32[256,512]{1,0:T(8,128)S(1)}, f32[256,512]{1,0:T(8,128)S(1)}, u32[]{:S(2)}, u32[]{:S(2)}) %collective-permute-start.6) | collective-permute-done | bytes 524320 | tf_op jit(solution)/shard_map/ppermute | solution.py:19
  222.6 0.1 maximum_select_fusion.4
  222.7 1.1 fusion.15
  223.8 1.1 fusion.47
  224.8 1.1 multiply_subtract_fusion
  225.9 1.9 collective-permute-start.7
  227.9 8.0 %collective-permute-done.7 = f32[256,512]{1,0:T(8,128)} collective-permute-done((f32[256,512]{1,0:T(8,128)S(1)}, f32[256,512]{1,0:T(8,128)}, u32[]{:S(2)}, u32[]{:S(2)}) %collective-permute-start.7) | collective-permute-done | bytes 524320 | tf_op jit(solution)/shard_map/ppermute | solution.py:19
  236.0 2.3 convolution_multiply_fusion.7
  238.3 3.2 %convolution_multiply_fusion = f32[512,1024]{1,0:T(8,128)} fusion(f32[128,512]{1,0:T(8,128)S(1)} %convolution_multiply_fusion.7, f32[128,1024]{1,0:T(8,128)S(1)} %bitcast.81), kind=kOutput, calls=%fused_computation.2 | convolution fusion | flops 805830656 | bytes 2883584 | tf_op jit(solution)/shard_map/dot_general | solution.py:83
  241.5 0.1 reshape.81
  241.6 60.2 %reduce-scatter.2.cloned.1.call-done = f32[64,1024]{1,0:T(8,128)} async-done(((f32[512,1024]{1,0:T(8,128)}), f32[64,1024]{1,0:T(8,128)}) %reduce-scatter.2.cloned.1.call-update) | async-done | bytes 262160 | tf_op jit(solution)/shard_map/reduce_scatter | solution.py:82
  301.9 1.2 reshape.82
  303.0 0.7 broadcast_select_fusion
  (22 shorter events, 0.6 us)
Async XLA Ops:
  6.5 60.3 %copy-start = (f32[1024,512]{1,0:T(8,128)S(1)}, f32[1024,512]{1,0:T(8,128)}, u32[]{:S(2)}) copy-start(f32[1024,512]{1,0:T(8,128)} %param.7) | copy-start | bytes 6291460
  6.5 50.9 %all-gather.2.cloned.1.call-start = ((), (), s32[]{:S(2)}) async-start(), calls=%async_computation.1 | async-start | bytes 2359296 | tf_op jit(solution)/shard_map/all_gather | solution.py:60
  6.5 8.1 %collective-permute-start = (f32[1,64,2,512]{3,2,1,0:T(2,128)}, f32[1,64,2,512]{3,2,1,0:T(2,128)S(1)}, u32[]{:S(2)}, u32[]{:S(2)}) collective-permute-start(f32[1,64,2,512]{3,2,1,0:T(2,128)} %param.5), channel_id=1, source_target_pairs={{0,8},{8,0},{16,24},{24,16},{32,40},{40,32},{48,56},{56,48},{64,72... | collective-permute-start | bytes 786440 | tf_op jit(solution)/shard_map/ppermute | solution.py:19
  16.6 130.0 %all-reduce.2.cloned.1.call-start = ((), (), s32[]{:S(2)}) async-start(), calls=%async_computation.2 | async-start | bytes 2097152 | tf_op jit(solution)/shard_map/psum | solution.py:67
  16.6 4.8 %collective-permute-start.1 = (f32[1,2]{1,0:T(1,128)}, f32[1,2]{1,0:T(1,128)S(1)}, u32[]{:S(2)}, u32[]{:S(2)}) collective-permute-start(f32[1,2]{1,0:T(1,128)} %param.6), channel_id=1, source_target_pairs={{0,8},{8,0},{16,24},{24,16},{32,40},{40,32},{48,56},{56,48},{64,72... | collective-permute-start | bytes 32 | tf_op jit(solution)/shard_map/ppermute | solution.py:19
  70.2 231.7 %reduce-scatter.2.cloned.1.call-start = ((), (), s32[]{:S(2)}) async-start(), calls=%async_computation.3 | async-start | bytes 2359296 | tf_op jit(solution)/shard_map/reduce_scatter | solution.py:82
  151.3 14.4 %copy-start.1 = (f32[512,512]{1,0:T(8,128)S(1)}, f32[512,512]{1,0:T(8,128)}, u32[]{:S(2)}) copy-start(f32[512,512]{1,0:T(8,128)} %all-reduce.2.cloned.1.call-done) | copy-start | bytes 3145732
  152.5 13.1 %collective-permute-start.2 = (f32[256,512]{1,0:T(8,128)S(1)}, f32[256,512]{1,0:T(8,128)S(1)}, u32[]{:S(2)}, u32[]{:S(2)}) collective-permute-start(f32[256,512]{1,0:T(8,128)S(1)} %fusion.5), channel_id=1, source_target_pairs={{0,8},{8,0},{16,24},{24,16},{32,40},{40,32},{48,56},{56,48},{64,72... | collective-permute-start | bytes 1572872 | tf_op jit(solution)/shard_map/ppermute | solution.py:19
  168.9 12.1 %collective-permute-start.3 = (f32[256,512]{1,0:T(8,128)S(1)}, f32[256,512]{1,0:T(8,128)S(1)}, u32[]{:S(2)}, u32[]{:S(2)}) collective-permute-start(f32[256,512]{1,0:T(8,128)S(1)} %multiply_subtract_fusion.4), channel_id=1, source_target_pairs={{0,8},{8,0},{16,24},{24,16},{32,40},{40,32},{48,56},{56,48},{64,72... | collective-permute-start | bytes 1572872 | tf_op jit(solution)/shard_map/ppermute | solution.py:19
  184.4 11.2 %collective-permute-start.4 = (f32[256,512]{1,0:T(8,128)S(1)}, f32[256,512]{1,0:T(8,128)S(1)}, u32[]{:S(2)}, u32[]{:S(2)}) collective-permute-start(f32[256,512]{1,0:T(8,128)S(1)} %multiply_subtract_fusion.3), channel_id=1, source_target_pairs={{0,8},{8,0},{16,24},{24,16},{32,40},{40,32},{48,56},{56,48},{64,72... | collective-permute-start | bytes 1572872 | tf_op jit(solution)/shard_map/ppermute | solution.py:19
  199.0 10.3 %collective-permute-start.5 = (f32[256,512]{1,0:T(8,128)S(1)}, f32[256,512]{1,0:T(8,128)S(1)}, u32[]{:S(2)}, u32[]{:S(2)}) collective-permute-start(f32[256,512]{1,0:T(8,128)S(1)} %multiply_subtract_fusion.2), channel_id=1, source_target_pairs={{0,8},{8,0},{16,24},{24,16},{32,40},{40,32},{48,56},{56,48},{64,72... | collective-permute-start | bytes 1572872 | tf_op jit(solution)/shard_map/ppermute | solution.py:19
  212.6 9.9 %collective-permute-start.6 = (f32[256,512]{1,0:T(8,128)S(1)}, f32[256,512]{1,0:T(8,128)S(1)}, u32[]{:S(2)}, u32[]{:S(2)}) collective-permute-start(f32[256,512]{1,0:T(8,128)S(1)} %multiply_subtract_fusion.1), channel_id=1, source_target_pairs={{0,8},{8,0},{16,24},{24,16},{32,40},{40,32},{48,56},{56,48},{64,72... | collective-permute-start | bytes 1572872 | tf_op jit(solution)/shard_map/ppermute | solution.py:19
  225.9 2.0 copy-start.2
  225.9 10.0 %collective-permute-start.7 = (f32[256,512]{1,0:T(8,128)S(1)}, f32[256,512]{1,0:T(8,128)}, u32[]{:S(2)}, u32[]{:S(2)}) collective-permute-start(f32[256,512]{1,0:T(8,128)S(1)} %multiply_subtract_fusion), channel_id=1, source_target_pairs={{0,8},{8,0},{16,24},{24,16},{32,40},{40,32},{48,56},{56,48},{64,72... | collective-permute-start | bytes 1572872 | tf_op jit(solution)/shard_map/ppermute | solution.py:19
Sparse Core Ops, SparseCore 0:
  16.7 40.6 all-gather.1
  70.3 76.1 all-reduce.1
  241.6 60.2 reduce-scatter.1
where the time goes:
time: 312 us; the launch traced here: 310 us
  waiting for transfers between devices  224 us (72%)
  matrix products  33.4 us (11%)
  starting transfers between devices  20.6 us (7%)
  between operations  18.3 us (6%)
  local copies, waits for them, and re-layouts  7.26 us (2%)
  other arithmetic  6.41 us (2%)
    psum x1, waiting for transfers between devices, per_device(): gram = lax.psum(jnp.dot(sketched.T, sketched, precision=HIGH), 'rows')  76.2 us
    reduce_scatter x1, waiting for transfers between devices, per_device(): lax.psum_scatter(jnp.dot(basis.T, theta, precision=HIGH) / (2.0 * width),...  60.2 us
    ppermute x8, waiting for transfers between devices, from_partner(): return lax.ppermute(block, axis, route)  59 us
    all_gather x1, waiting for transfers between devices, per_device(): lax.all_gather(right_mat, 'rows', axis=0, tiled=True)  28.9 us
    ppermute x8, starting transfers between devices, from_partner(): return lax.ppermute(block, axis, route)  20.5 us
    dot_general x6, matrix products, refine(): jnp.dot(own, normed, precision=HIGH)  7.38 us
  transfers between devices with their start and end apart: 11, of which 11 were waited for; matrix products, arithmetic and copies ran while one was open for 1% of the time, Pallas kernels for 0%

commit v1 on v0

v1 whole, which is shorter than its diff:
```python
import functools

import jax
import jax.numpy as jnp
from jax import lax
from jax.experimental import pallas as pl
from jax.experimental.pallas import tpu as pltpu
from jax.sharding import PartitionSpec as P

ITERS = 6
MESH = pl.DeviceIdType.MESH
F32 = jnp.float32
BF16 = jnp.bfloat16

GA, GS, GL = 0, 1, 2
PRI, SEC, FWD, B0, B1, B2, B3 = range(7)


def split(x):
    high = x.astype(BF16)
    return high, (x - high.astype(F32)).astype(BF16)


def dot3(a, b, contract=((1,), (0,))):
    ah, al = a
    bh, bl = b
    d = functools.partial(
        lax.dot_general, dimension_numbers=(contract, ((), ())), preferred_element_type=F32
    )
    return d(ah, bh) + (d(ah, bl) + d(al, bh))


def kernel(
    sites, angles, sketch, out,
    buf, lbuf, sbuf, wbuf, wh, wl, zf, zh, zl, ah, al, xbuf, obuf, ang,
    ss, rs, vs, vr, bs, br, loc,
):
    chain = lax.axis_index("chain")
    row = lax.axis_index("rows")
    parity = lax.rem(chain, 2)
    core = lax.rem(row, 2)
    place = lax.div(row, 2)
    half = sites.shape[1]
    width = sites.shape[3]
    turn = 1 - 2 * core
    xs = lax.axis_size("rows") // 2

    def at(step):
        return lax.rem(place + step + xs, xs)

    ahead, behind, across = at(turn), at(-turn), at(2)
    dev_ahead = (chain, 2 * ahead + core)
    dev_behind = (chain, 2 * behind + core)
    dev_sib = (chain, 2 * place + 1 - core)
    dev_y = (chain + 1 - 2 * parity, row)
    blk_own, blk_behind, blk_ahead, blk_across = (
        row, 2 * behind + core, 2 * ahead + core, 2 * across + core,
    )
    sib_own, sib_behind, sib_ahead, sib_across = (
        2 * place + 1 - core, 2 * behind + 1 - core, 2 * ahead + 1 - core, 2 * across + 1 - core,
    )

    def rows(block):
        return pl.ds(pl.multiple_of(half * block, half), half)

    barrier = pltpu.get_barrier_semaphore()
    for device in (dev_ahead, dev_behind, dev_sib, dev_y):
        pl.semaphore_signal(barrier, inc=1, device_id=device, device_id_type=MESH)

    def remote(src, dst, send, recv, device):
        return pltpu.make_async_remote_copy(
            src_ref=src, dst_ref=dst, send_sem=send, recv_sem=recv,
            device_id=device, device_id_type=MESH,
        )

    def piece(which, kind, c, view, block, device):
        ref = view.at[c, rows(block)]
        return remote(ref, ref, ss.at[which, kind, c], rs.at[which, kind, c], device)

    sends = {
        PRI: (blk_own, dev_ahead), SEC: (blk_own, dev_behind), FWD: (blk_behind, dev_ahead),
        B0: (blk_own, dev_sib), B1: (blk_behind, dev_sib),
        B2: (blk_ahead, dev_sib), B3: (blk_across, dev_sib),
    }
    gets = {
        PRI: blk_behind, SEC: blk_ahead, FWD: blk_across,
        B0: sib_own, B1: sib_ahead, B2: sib_behind, B3: sib_across,
    }

    def send(which, kind, view, chunks=(0, 1)):
        for c in chunks:
            piece(which, kind, c, view, *sends[kind]).start()

    def get(which, kind, view, chunks=(0, 1)):
        for c in chunks:
            piece(which, kind, c, view, gets[kind], dev_sib).wait_recv()

    def drain(which, kinds, view):
        for kind in kinds:
            for c in range(2):
                piece(which, kind, c, view, *sends[kind]).wait_send()

    raw, proj = buf.at[0], buf.at[1]
    ring = buf.at[1 - parity]

    def own_copy(view, s):
        return pltpu.make_async_copy(sites.at[0, :, s], view.at[s, rows(blk_own)], loc.at[s])

    def rsib(c, block):
        ref = raw.at[c, rows(block)]
        return ref

    def load_sites(view):
        for s in range(2):
            own_copy(view, s).start()
        for s in range(2):
            own_copy(view, s).wait()

    for n in range(2):
        ang[parity, 8 * n : 8 * n + 8, :] = jnp.full((8, 128), angles[0, n], F32)

    def project(block):
        kick = ang[1, 0:8, :]
        cb, sb = jnp.cos(kick)[0:1, 0:1], jnp.sin(kick)[0:1, 0:1]
        r0, r1 = raw[0, rows(block), :], raw[1, rows(block), :]
        p, q = cb * r0 - sb * r1, sb * r0 + cb * r1
        u, v = cb * r1 - sb * r0, cb * r0 + sb * r1
        lhs = jnp.concatenate(
            [jnp.concatenate([p, q], 1), jnp.concatenate([u, v], 1)], 0
        )
        result = dot3(split(lhs), (wh[...], wl[...]))
        proj[0, rows(block), :] = result[:half]
        proj[1, rows(block), :] = result[half:]

    @pl.when(parity == 0)
    def _():
        load_sites(lbuf)

    @pl.when(parity == 1)
    def _():
        fetch = pltpu.make_async_copy(sketch, wbuf, loc.at[2])
        fetch.start()
        load_sites(raw)
        fetch.wait()
        high, low = split(wbuf[...])
        wh[...] = high
        wl[...] = low
        project(blk_own)

    pl.semaphore_wait(barrier, 4)

    def ang_copy(site):
        return remote(ang.at[site], ang.at[site], vs.at[4], vr.at[4], dev_y)

    def over_y(c, view):
        ref = view.at[c, rows(blk_own)]
        return remote(ref, ref, vs.at[c], vr.at[c], dev_y)

    @pl.when(parity == 1)
    def _():
        send(GA, PRI, ring)
        for c in range(2):
            over_y(c, proj).start()
        send(GA, SEC, ring)
        send(GA, B0, proj)
        ang_copy(parity).start()

    @pl.when(parity == 0)
    def _():
        ang_copy(parity).start()
        for c in range(2):
            over_y(c, lbuf).start()
        for c in range(2):
            over_y(c, proj).wait_recv()
            send(GA, PRI, ring, (c,))
            send(GA, SEC, ring, (c,))
            send(GA, B0, proj, (c,))

    def arrived(kind, then, block, passed):
        for c in range(2):
            get(GA, kind, ring, (c,))
            for other, view in then:
                send(GA, other, view, (c,))

        @pl.when(parity == 1)
        def _():
            project(block)

        send(GA, passed, proj)

    arrived(PRI, [(FWD, ring)], blk_behind, B1)
    arrived(SEC, [], blk_ahead, B2)
    arrived(FWD, [], blk_across, B3)

    ang_copy(1 - parity).wait_recv()

    @pl.when(parity == 1)
    def _():
        for c in range(2):
            over_y(c, lbuf).wait_recv()

    kick, turn_l, turn_r = ang[0, 0:8, :], ang[0, 8:16, :], ang[1, 8:16, :]
    coupling = 0.5 * (turn_l + turn_r)
    ca, sa = jnp.cos(kick)[0:1, 0:1], jnp.sin(kick)[0:1, 0:1]
    cj, sj = jnp.cos(coupling)[0:1, 0:1], jnp.sin(coupling)[0:1, 0:1]
    l0, l1 = lbuf[0, rows(blk_own), :], lbuf[1, rows(blk_own), :]
    p, q = ca * l0 - sa * l1, sa * l0 + ca * l1
    lhs = jnp.concatenate(
        [jnp.concatenate([cj * p, sj * q], 1), jnp.concatenate([cj * q, -sj * p], 1)], 0
    )
    for kind in (B0, B1, B2, B3):
        get(GA, kind, proj)
    own = dot3(split(lhs), split(proj[...].reshape(2 * width, width)))
    sbuf[0, rows(blk_own), :] = own[:half]
    sbuf[1, rows(blk_own), :] = own[half:]

    for c in range(2):
        send(GS, PRI, sbuf, (c,))
    for c in range(2):
        send(GS, SEC, sbuf, (c,))
    send(GS, B0, sbuf)
    for kind, then in ((PRI, (FWD, B1)), (SEC, (B2,)), (FWD, (B3,))):
        for c in range(2):
            get(GS, kind, sbuf, (c,))
            for other in then:
                send(GS, other, sbuf, (c,))
    def sibling_r(n, c, block):
        ref = raw.at[c, rows(block)]
        return remote(ref, ref, bs.at[n, c], br.at[n, c], dev_sib)

    own_blocks = (blk_own, blk_behind, blk_ahead, blk_across)
    sib_blocks = (sib_own, sib_ahead, sib_behind, sib_across)

    @pl.when(parity == 1)
    def _():
        send(GL, PRI, lbuf)
        send(GL, SEC, lbuf)
        send(GL, B0, lbuf)

    for kind in (B0, B1, B2, B3):
        get(GS, kind, sbuf)

    stacked = split(sbuf[...].reshape(2 * width, width))
    gram = dot3(stacked, stacked, ((0,), (0,)))
    scale = jnp.sqrt(jnp.sum(gram * gram, keepdims=True).reshape(1, 1) + 1e-06)
    zf[...] = gram / scale
    at_row = lax.broadcasted_iota(jnp.int32, (2 * half, width), 0)
    at_col = lax.broadcasted_iota(jnp.int32, (2 * half, width), 1)
    unit = jnp.where((at_col == at_row + half * row) & (at_row < half), 1.0, 0.0).astype(F32)
    xbuf[...] = jnp.where(parity == 0, own, unit)

    def refine(step, carry):
        z = zf[...]
        x = xbuf[...]
        z2 = split(z)
        x2 = split(x)
        lhs2 = tuple(jnp.concatenate([a, b], 0) for a, b in zip(z2, x2))
        both = dot3(lhs2, z2)
        square, moved = both[:width], both[width:]
        xbuf[...] = 1.5 * x - 0.5 * moved
        cube = dot3(split(square), z2)
        zf[...] = 2.25 * z - 1.5 * square + 0.25 * cube

        @pl.when((parity == 1) & (step == 0))
        def _():
            for n, block in enumerate(own_blocks):
                for c in range(2):
                    sibling_r(n, c, block).start()

        @pl.when((parity == 1) & (step == 2))
        def _():
            get(GL, PRI, lbuf)
            send(GL, FWD, lbuf)
            send(GL, B1, lbuf)

        @pl.when((parity == 1) & (step == 3))
        def _():
            get(GL, SEC, lbuf)
            send(GL, B2, lbuf)

        @pl.when((parity == 1) & (step == ITERS - 2))
        def _():
            get(GL, FWD, lbuf)
            send(GL, B3, lbuf)

        return carry

    lax.fori_loop(0, ITERS - 1, refine, 0)
    x = xbuf[...]
    x = 1.5 * x - 0.5 * dot3(split(x), split(zf[...]))

    gain = jnp.sqrt(2.0 * width / scale)

    @pl.when(parity == 0)
    def _():
        obuf[...] = (x * gain).reshape(2, half, width)

    @pl.when(parity == 1)
    def _():
        for kind in (B0, B1, B2, B3):
            get(GL, kind, lbuf)
        for n, block in enumerate(sib_blocks):
            for c in range(2):
                sibling_r(n, c, block).wait_recv()
        cols = split(x[:half] * gain)
        e0 = dot3(cols, split(sbuf[0]), ((1,), (1,)))
        e1 = dot3(cols, split(sbuf[1]), ((1,), (1,)))
        f, g = ca * e0 + sa * e1, ca * e1 - sa * e0
        lhs = jnp.concatenate(
            [jnp.concatenate([cj * f, cj * g], 1), jnp.concatenate([-sj * g, sj * f], 1)], 0
        )
        core_mat = dot3(split(lhs), split(lbuf[...].reshape(2 * width, width)))
        c0, c1 = core_mat[:half], core_mat[half:]
        kick_r = ang[1, 0:8, :]
        cb, sb = jnp.cos(kick_r)[0:1, 0:1], jnp.sin(kick_r)[0:1, 0:1]
        k00, k01 = cb * c0 - sb * c1, cb * c1 - sb * c0
        k10, k11 = sb * c0 + cb * c1, cb * c0 + sb * c1
        lhs = jnp.concatenate(
            [jnp.concatenate([k00, k01], 1), jnp.concatenate([k10, k11], 1)], 0
        )
        right = dot3(split(lhs), split(raw[...].reshape(2 * width, width)))
        obuf[...] = (right * (1.0 / (2.0 * width))).reshape(2, half, width)

    stores = [
        pltpu.make_async_copy(obuf.at[s], out.at[0, :, s], loc.at[s]) for s in range(2)
    ]
    for store in stores:
        store.start()

    ang_copy(parity).wait_send()

    @pl.when(parity == 0)
    def _():
        for c in range(2):
            over_y(c, lbuf).wait_send()

    @pl.when(parity == 1)
    def _():
        for c in range(2):
            over_y(c, proj).wait_send()
        drain(GL, range(7), lbuf)
        for n, block in enumerate(own_blocks):
            for c in range(2):
                sibling_r(n, c, block).wait_send()

    drain(GA, (PRI, SEC, FWD), ring)
    drain(GA, (B0, B1, B2, B3), proj)
    drain(GS, range(7), sbuf)
    for store in stores:
        store.wait()


def per_device(sites, angles, sketch):
    half, width = sites.shape[1], sites.shape[3]
    dma = pltpu.SemaphoreType.DMA
    return pl.pallas_call(
        kernel,
        out_shape=jax.ShapeDtypeStruct(sites.shape, F32),
        in_specs=[
            pl.BlockSpec(memory_space=pl.ANY),
            pl.BlockSpec(memory_space=pltpu.SMEM),
            pl.BlockSpec(memory_space=pl.ANY),
        ],
        out_specs=pl.BlockSpec(memory_space=pl.ANY),
        scratch_shapes=[
            pltpu.VMEM((2, 2, width, width), F32),
            pltpu.VMEM((2, width, width), F32),
            pltpu.VMEM((2, width, width), F32),
            pltpu.VMEM((2 * width, width), F32),
            pltpu.VMEM((2 * width, width), BF16),
            pltpu.VMEM((2 * width, width), BF16),
            pltpu.VMEM((width, width), F32),
            pltpu.VMEM((width, width), BF16),
            pltpu.VMEM((width, width), BF16),
            pltpu.VMEM((width + 2 * half, width), BF16),
            pltpu.VMEM((width + 2 * half, width), BF16),
            pltpu.VMEM((2 * half, width), F32),
            pltpu.VMEM((2, half, width), F32),
            pltpu.VMEM((2, 16, 128), F32),
            dma((3, 7, 2)), dma((3, 7, 2)),
            dma((5,)), dma((5,)),
            dma((4, 2)), dma((4, 2)),
            dma((3,)),
        ],
        compiler_params=pltpu.CompilerParams(
            collective_id=0, has_side_effects=True, vmem_limit_bytes=56 * 2**20
        ),
        cost_estimate=pl.CostEstimate(
            flops=20 * 6 * width**3, bytes_accessed=3 * 2**20, transcendentals=0
        ),
    )(sites, angles, sketch)


def solution(mesh):
    in_specs = (P("chain", "rows", None, None), P("chain", None), P())
    out_specs = P("chain", "rows", None, None)
    return jax.shard_map(
        per_device, mesh=mesh, in_specs=in_specs, out_specs=out_specs, check_vma=False
    )
```

time: 312 us -> 53.5 us (0.17)
  waiting for transfers between devices: 224 us -> 0 us
  Pallas kernels: 0 us -> 51.6 us
  matrix products: 33.4 us -> 0 us
  starting transfers between devices: 20.6 us -> 0 us
  between operations: 18.3 us -> 0.01 us
  other arithmetic: 6.41 us -> 0 us
  local copies, waits for them, and re-layouts: 7.26 us -> 1.67 us
    psum x1 -> x0, waiting for transfers between devices: 76.2 us -> none  [per_device(): gram = lax.psum(jnp.dot(sketched.T, sketched, precision=HIGH), 'rows')]
    reduce_scatter x1 -> x0, waiting for transfers between devices: 60.2 us -> none  [per_device(): lax.psum_scatter(jnp.dot(basis.T, theta, precision=HIGH) / (2.0 * width),...]
    ppermute x8 -> x0, waiting for transfers between devices: 59 us -> none  [from_partner(): return lax.ppermute(block, axis, route)]
    pallas_call x0 -> x1, Pallas kernels: none -> 51.6 us  [per_device(): pl.pallas_call(kernel, out_shape=jax.ShapeDtypeStruct(sites.shape, F32),...]
    dot_general x25 -> x0, matrix products: 33.4 us -> none  [the longest x6 7.38 us: refine(): jnp.dot(own, normed, precision=HIGH)]
    all_gather x1 -> x0, waiting for transfers between devices: 28.9 us -> none  [per_device(): lax.all_gather(right_mat, 'rows', axis=0, tiled=True)]
    ppermute x8 -> x0, starting transfers between devices: 20.5 us -> none  [from_partner(): return lax.ppermute(block, axis, route)]
    dot_general x2 -> x0, local copies, waits for them, and re-layouts: 4.1 us -> none  [the longest x1 4 us: per_device(): jnp.dot(left_mat, lax.all_gather(right_mat, 'rows', axis=0, tiled=True),...]
  transfers between devices with their start and end apart: 11 -> 0, of which waited for: 11 -> 0; matrix products, arithmetic and copies ran while one was open for 1% -> 0% of each run, Pallas kernels for 0% -> 0%
where the time goes in v1:
time: 53.5 us; the launch traced here: 53.3 us
  Pallas kernels  51.6 us (96%)
  local copies, waits for them, and re-layouts  1.67 us (3%)
    pallas_call x1, Pallas kernels, per_device(): pl.pallas_call(kernel, out_shape=jax.ShapeDtypeStruct(sites.shape, F32),...  51.6 us
    unnamed x1, local copies, waits for them, and re-layouts  1.67 us

profile of v1, /device:TPU:1, one launch (start us, length us, event | category | flops | bytes accessed | tf_op | source)
XLA Modules:
  0.0 53.3 jit_solution(7764831630443346912)
XLA Ops:
  0.0 51.6 %shard_map.37 = f32[1,64,2,512]{3,2,1,0:T(2,128)} custom-call(f32[1,64,2,512]{3,2,1,0:T(2,128)} %sites.1, f32[1,2]{1,0:T(1,128)} %angles.1, f32[1024,512]{1,0:T(8,128)} %sketch.1), custom_call_target="tpu_custom_call" | custom-call | flops 16106127360 | bytes 3145728 | tf_op jit(solution)/shard_map/pallas_call | solution.py:356
  51.6 1.7 %copy.5 = f32[1,64,2,512]{3,2,1,0:T(2,128)} copy(f32[1,64,2,512]{3,2,1,0:T(2,128)} %shard_map.37) | data formatting | bytes 524288

commit v2 on v0

v2 whole, which is shorter than its diff:
```python
import functools

import jax
import jax.numpy as jnp
from jax import lax
from jax.experimental import pallas as pl
from jax.experimental.pallas import tpu as pltpu
from jax.sharding import PartitionSpec as P

ITERS = 6
MESH = pl.DeviceIdType.MESH
F32 = jnp.float32
BF16 = jnp.bfloat16
CUT = 128

RP, RM, FW, B0, BM, BP, BX = range(7)
G_RWA, G_RWB, G_SA, G_SB, G_R, G_L = range(6)
Y_RW, Y_SB, Y_ANG, Y_L = range(4)


def split(x):
    high = x.astype(BF16)
    return high, (x - high.astype(F32)).astype(BF16)


def dot3(a, b, contract=((1,), (0,))):
    ah, al = a
    bh, bl = b
    d = functools.partial(
        lax.dot_general, dimension_numbers=(contract, ((), ())), preferred_element_type=F32
    )
    return d(ah, bh) + (d(ah, bl) + d(al, bh))


def beside(*parts):
    return jnp.concatenate(parts, 1)


def above(*parts):
    return jnp.concatenate(parts, 0)


def kernel(
    sites, angles, sketch, out,
    raw, lbuf, rwa, rwb, sa_, sb_, wbuf, wh, wl, zf, xbuf, obuf, ang, trig,
    ss, rs, vs, vr, loc,
):
    chain = lax.axis_index("chain")
    row = lax.axis_index("rows")
    parity = lax.rem(chain, 2)
    core = lax.rem(row, 2)
    place = lax.div(row, 2)
    half, width = sites.shape[1], sites.shape[3]
    xs = lax.axis_size("rows") // 2
    is_left, is_right = parity == 0, parity == 1

    def at(step):
        return lax.rem(place + step + xs, xs)

    plus, minus, across = at(1), at(-1), at(2)
    dev_plus = (chain, 2 * plus + core)
    dev_minus = (chain, 2 * minus + core)
    dev_sib = (chain, 2 * place + 1 - core)
    dev_y = (chain + 1 - 2 * parity, row)

    barrier = pltpu.get_barrier_semaphore()
    for device in (dev_plus, dev_minus, dev_sib, dev_y):
        pl.semaphore_signal(barrier, inc=1, device_id=device, device_id_type=MESH)

    def rows(block):
        return pl.ds(pl.multiple_of(half * block, half), half)

    own = rows(row)

    def chunk(view, block, c, count):
        part = 2 * half // count
        start = half * block + part * (c % (count // 2))
        return view.at[c // (count // 2), pl.ds(pl.multiple_of(start, part), part)]

    def remote(ref, send, recv, device):
        return pltpu.make_async_remote_copy(
            src_ref=ref, dst_ref=ref, send_sem=send, recv_sem=recv,
            device_id=device, device_id_type=MESH,
        )

    blk_minus, blk_plus, blk_across = (2 * n + core for n in (minus, plus, across))
    sib_own, sib_minus, sib_plus, sib_across = (
        2 * n + 1 - core for n in (place, minus, plus, across)
    )
    sends = {
        RP: (row, dev_plus), RM: (row, dev_minus), B0: (row, dev_sib),
        BM: (blk_minus, dev_sib), BP: (blk_plus, dev_sib), BX: (blk_across, dev_sib),
    }
    gets = {
        RP: blk_minus, RM: blk_plus, FW: blk_across,
        B0: sib_own, BM: sib_minus, BP: sib_plus, BX: sib_across,
    }

    class Ring:
        def __init__(self, view, which, count, shared=True):
            self.view, self.which, self.count, self.shared = view, which, count, shared
            self.low, self.high = range(count // 2), range(count // 2, count)

        def copy(self, kind, c, block, device):
            ref = chunk(self.view, block, c, self.count)
            return remote(ref, ss.at[self.which, kind, c], rs.at[self.which, kind, c], device)

        def sent(self, kind, c):
            if kind == FW:
                passed = (blk_minus, dev_plus) if c in self.low else (blk_plus, dev_minus)
                return self.copy(FW, c, *passed)
            return self.copy(kind, c, *sends[kind])

        def send(self, kind, c):
            self.sent(kind, c).start()

        def get(self, kind, c):
            self.copy(kind, c, gets[kind], dev_sib).wait_recv()

        def issue(self):
            for c, d in zip(self.low, self.high):
                self.send(RP, c)
                self.send(RM, d)
            for c, d in zip(self.low, self.high):
                self.send(RP, d)
                self.send(RM, c)
            self.share(B0)

        def share(self, kind):
            if self.shared:
                for c in range(self.count):
                    self.send(kind, c)

        def issue_chunk(self, c):
            for kind in (RP, RM, B0):
                self.send(kind, c)

        def step1(self):
            for c, d in zip(self.low, self.high):
                self.get(RP, c)
                self.send(FW, c)
                self.get(RM, d)
                self.send(FW, d)
                if self.shared:
                    self.send(BM, c)
                    self.send(BP, d)

        def step2(self):
            for c, d in zip(self.low, self.high):
                self.get(RP, d)
                self.get(RM, c)
                if self.shared:
                    self.send(BM, d)
                    self.send(BP, c)

        def step3(self):
            for c, d in zip(self.low, self.high):
                for n in (c, d):
                    self.get(FW, n)
                    if self.shared:
                        self.send(BX, n)

        def finish(self, *kinds):
            for kind in kinds:
                for c in range(self.count):
                    self.get(kind, c)

        def drain(self, kinds=range(7)):
            for kind in kinds:
                for c in range(self.count):
                    self.sent(kind, c).wait_send()

    ring_rwa, ring_rwb = Ring(rwa, G_RWA, 2), Ring(rwb, G_RWB, 4)
    ring_sa, ring_sb = Ring(sa_, G_SA, 2), Ring(sb_, G_SB, 4)
    ring_r, ring_l = Ring(raw, G_R, 4), Ring(lbuf, G_L, 4, shared=False)
    chip_l = Ring(lbuf, G_L, 4)

    def over_y(view, which, c, count, block=row):
        return remote(chunk(view, block, c, count), vs.at[which, c], vr.at[which, c], dev_y)

    l_blocks = (row, blk_minus, blk_plus, blk_across)

    def l_over_y(n, c):
        return over_y(lbuf, Y_L + n, c, 4, l_blocks[n])

    def ang_copy(site):
        return remote(ang.at[site], vs.at[Y_ANG, 0], vr.at[Y_ANG, 0], dev_y)

    def load_sites(view):
        copies = [
            pltpu.make_async_copy(sites.at[0, :, s], view.at[s, own], loc.at[s]) for s in range(2)
        ]
        for copy in copies:
            copy.start()
        for copy in copies:
            copy.wait()

    for n in range(2):
        ang[parity, 8 * n : 8 * n + 8, :] = jnp.full((8, 128), angles[0, n], F32)

    def scalar(n):
        return trig[n, 0:1, 0:1]

    @pl.when(is_left)
    def _():
        load_sites(lbuf)

    @pl.when(is_right)
    def _():
        fetch = pltpu.make_async_copy(sketch, wbuf, loc.at[2])
        fetch.start()
        load_sites(raw)
        kick = ang[1, 0:8, :]
        trig[4] = jnp.cos(kick)
        trig[5] = jnp.sin(kick)
        cb, sb = scalar(4), scalar(5)
        r0, r1 = raw[0, own, :], raw[1, own, :]
        mixed = above(
            beside(cb * r0 - sb * r1, sb * r0 + cb * r1),
            beside(cb * r1 - sb * r0, cb * r0 + sb * r1),
        )
        fetch.wait()
        high, low = split(wbuf[...])
        wh[...] = high
        wl[...] = low
        result = dot3(split(mixed), (wh[...], wl[...]))
        for m in range(2):
            rwa[m, own, :] = result[half * m : half * (m + 1), :CUT]
            rwb[m, own, :] = result[half * m : half * (m + 1), CUT:]

    pl.semaphore_wait(barrier, 4)

    def all_trig():
        ang_copy(1 - parity).wait_recv()
        kick, coupling = ang[0, 0:8, :], 0.5 * (ang[0, 8:16, :] + ang[1, 8:16, :])
        trig[0] = jnp.cos(kick)
        trig[1] = jnp.sin(kick)
        trig[2] = jnp.cos(coupling)
        trig[3] = jnp.sin(coupling)

    def rows_of_s(view, into):
        ca, sa, cj, sj = (scalar(n) for n in range(4))
        l0, l1 = lbuf[0, own, :], lbuf[1, own, :]
        p, q = ca * l0 - sa * l1, sa * l0 + ca * l1
        lhs = above(beside(cj * p, sj * q), beside(cj * q, -sj * p))
        result = dot3(split(lhs), split(view[...].reshape(2 * width, view.shape[2])))
        for s in range(2):
            into[s, own, :] = result[half * s : half * (s + 1)]

    @pl.when(is_right)
    def _():
        ang_copy(parity).start()
        for c in range(2):
            over_y(rwa, Y_RW, c, 2).start()
        ring_rwb.issue()
        ring_rwb.step1()
        ring_rwa.issue()
        ring_rwb.step2()
        all_trig()
        for c in range(4):
            l_over_y(0, c).wait_recv()
        ring_rwa.step1()
        ring_rwb.step3()
        ring_rwb.finish(B0, BM, BP, BX)
        rows_of_s(rwb, sb_)
        for c in (0, 2, 1, 3):
            over_y(sb_, Y_SB, c, 4).start()
        ring_sb.issue()
        ring_rwa.step2()
        ring_rwa.step3()
        ring_rwa.finish(B0, BM, BP, BX)
        rows_of_s(rwa, sa_)
        ring_sa.issue()
        chip_l.share(B0)
        ring_sb.step1()
        ring_sa.step1()
        ring_sb.step2()
        ring_sa.step2()
        ring_r.issue()

    @pl.when(is_left)
    def _():
        ang_copy(parity).start()
        for c in range(4):
            l_over_y(0, c).start()
        ring_l.issue()
        for c in range(2):
            over_y(rwa, Y_RW, c, 2).wait_recv()
            ring_rwa.issue_chunk(c)
        all_trig()
        ring_rwa.step1()
        ring_l.step1()
        for c in range(2):
            l_over_y(1, c).start()
            l_over_y(2, c + 2).start()
        ring_rwa.step2()
        ring_rwa.step3()
        ring_rwa.finish(B0, BM, BP, BX)
        rows_of_s(rwa, sa_)
        ring_sa.issue()
        ring_l.step2()
        for c in range(2):
            l_over_y(1, c + 2).start()
            l_over_y(2, c).start()
        for c in (0, 2):
            over_y(sb_, Y_SB, c, 4).wait_recv()
            ring_sb.issue_chunk(c)
        ring_sa.step1()
        for c in (1, 3):
            over_y(sb_, Y_SB, c, 4).wait_recv()
            ring_sb.issue_chunk(c)
        ring_sa.step2()
        ring_sb.step1()
        ring_sa.step3()
        ring_l.step3()
        for c in range(4):
            l_over_y(3, c).start()

    cut = width // 2

    def add_gram(where, first=False):
        two = pl.ds(pl.multiple_of(2 * half * where, 2 * half), 2 * half)
        pair = split(above(*(beside(sa_[s, two, :], sb_[s, two, :]) for s in range(2))))
        right = tuple(n[:, cut:] for n in pair)
        top = dot3(tuple(n[:, :cut] for n in pair), pair, ((0,), (0,)))
        low = dot3(right, right, ((0,), (0,)))
        if first:
            zf[:cut, :] = top
            zf[cut:, cut:] = low
        else:
            zf[:cut, :] += top
            zf[cut:, cut:] += low

    def finish_s(*kinds):
        ring_sa.finish(*kinds)
        ring_sb.finish(*kinds)

    finish_s(B0)
    add_gram(place, first=True)

    @pl.when(is_right)
    def _():
        ring_sb.step3()

    @pl.when(is_left)
    def _():
        ring_sb.step2()

    finish_s(BM, BP)
    add_gram(minus)
    add_gram(plus)

    @pl.when(is_right)
    def _():
        ring_sa.step3()

    @pl.when(is_left)
    def _():
        ring_sb.step3()

    finish_s(BX)
    add_gram(across)
    zf[cut:, :cut] = zf[:cut, cut:].T
    gram = zf[...]
    scale = jnp.sqrt(jnp.sum(gram * gram, keepdims=True).reshape(1, 1) + 1e-06)
    zf[...] = gram / scale
    at_row = lax.broadcasted_iota(jnp.int32, (2 * half, width), 0)
    at_col = lax.broadcasted_iota(jnp.int32, (2 * half, width), 1)
    unit = jnp.where((at_col == at_row + half * row) & (at_row < half), 1.0, 0.0).astype(F32)
    mine = above(*(beside(sa_[s, own, :], sb_[s, own, :]) for s in range(2)))
    xbuf[...] = jnp.where(is_left, mine, unit)

    def refine(step, carry):
        z, x = zf[...], xbuf[...]
        z2, x2 = split(z), split(x)
        zr = tuple(n[:, cut:] for n in z2)
        both = dot3(tuple(above(a[:cut], b) for a, b in zip(z2, x2)), z2)
        top, moved = both[:cut], both[cut:]
        low = dot3(tuple(n[cut:] for n in z2), zr)
        xbuf[...] = 1.5 * x - 0.5 * moved
        top2, low2 = split(top), split(low)
        under = tuple(beside(a[:, cut:].T, b) for a, b in zip(top2, low2))
        new_top = 2.25 * z[:cut] - 1.5 * top + 0.25 * dot3(top2, z2)
        new_low = 2.25 * z[cut:, cut:] - 1.5 * low + 0.25 * dot3(under, zr)
        zf[:cut, :] = new_top
        zf[cut:, :cut] = new_top[:, cut:].T
        zf[cut:, cut:] = new_low

        @pl.when(is_right & (step == 0))
        def _():
            ring_r.step1()
            for n, kind in ((1, BM), (2, BP)):
                for c in range(4):
                    l_over_y(n, c).wait_recv()
                chip_l.share(kind)

        @pl.when(is_right & (step == 1))
        def _():
            ring_r.step2()

        @pl.when(is_right & (step == ITERS - 3))
        def _():
            ring_r.step3()
            for c in range(4):
                l_over_y(3, c).wait_recv()
            chip_l.share(BX)

        return carry

    lax.fori_loop(0, ITERS - 2, refine, 0)
    z2, x = split(zf[...]), xbuf[...]

    def times_z(rows_):
        return dot3(split(rows_), z2)

    moved = times_z(x)
    x = 1.5 * x - 0.5 * moved
    turned = 1.5 * moved - 0.5 * times_z(moved)
    for _ in range(2):
        turned = 1.5 * turned - 0.5 * times_z(turned)
    x = 1.5 * x - 0.5 * turned

    gain = jnp.sqrt(2.0 * width / scale)

    @pl.when(is_left)
    def _():
        obuf[...] = (x * gain).reshape(2, half, width)

    @pl.when(is_right)
    def _():
        chip_l.finish(B0, BM, BP, BX)
        ring_r.finish(B0, BM, BP, BX)
        ca, sa, cj, sj, cb, sb = (scalar(n) for n in range(6))
        cols = split(x[:half] * gain)
        e0, e1 = (
            dot3(cols, split(beside(sa_[s], sb_[s])), ((1,), (1,))) for s in range(2)
        )
        f, g = ca * e0 + sa * e1, ca * e1 - sa * e0
        lhs = above(beside(cj * f, cj * g), beside(-sj * g, sj * f))
        both = dot3(split(lhs), split(lbuf[...].reshape(2 * width, width)))
        c0, c1 = both[:half], both[half:]
        lhs = above(
            beside(cb * c0 - sb * c1, cb * c1 - sb * c0),
            beside(sb * c0 + cb * c1, cb * c0 + sb * c1),
        )
        right = dot3(split(lhs), split(raw[...].reshape(2 * width, width)))
        obuf[...] = (right * (1.0 / (2.0 * width))).reshape(2, half, width)

    stores = [
        pltpu.make_async_copy(obuf.at[s], out.at[0, :, s], loc.at[s]) for s in range(2)
    ]
    for store in stores:
        store.start()

    ang_copy(parity).wait_send()
    ring_rwa.drain()
    ring_sa.drain()
    ring_sb.drain()

    @pl.when(is_left)
    def _():
        for c in range(4):
            for n in range(4):
                l_over_y(n, c).wait_send()
        ring_l.drain((RP, RM, FW))

    @pl.when(is_right)
    def _():
        for c in range(2):
            over_y(rwa, Y_RW, c, 2).wait_send()
        for c in range(4):
            over_y(sb_, Y_SB, c, 4).wait_send()
        ring_rwb.drain()
        ring_r.drain()
        chip_l.drain((B0, BM, BP, BX))

    for store in stores:
        store.wait()


def per_device(sites, angles, sketch):
    half, width = sites.shape[1], sites.shape[3]
    dma, vmem = pltpu.SemaphoreType.DMA, pltpu.VMEM
    return pl.pallas_call(
        kernel,
        out_shape=jax.ShapeDtypeStruct(sites.shape, F32),
        in_specs=[
            pl.BlockSpec(memory_space=pl.ANY),
            pl.BlockSpec(memory_space=pltpu.SMEM),
            pl.BlockSpec(memory_space=pl.ANY),
        ],
        out_specs=pl.BlockSpec(memory_space=pl.ANY),
        scratch_shapes=[
            vmem((2, width, width), F32),
            vmem((2, width, width), F32),
            vmem((2, width, CUT), F32),
            vmem((2, width, width - CUT), F32),
            vmem((2, width, CUT), F32),
            vmem((2, width, width - CUT), F32),
            vmem((2 * width, width), F32),
            vmem((2 * width, width), BF16),
            vmem((2 * width, width), BF16),
            vmem((width, width), F32),
            vmem((2 * half, width), F32),
            vmem((2, half, width), F32),
            vmem((2, 16, 128), F32),
            vmem((6, 8, 128), F32),
            dma((6, 7, 4)), dma((6, 7, 4)),
            dma((7, 4)), dma((7, 4)),
            dma((3,)),
        ],
        compiler_params=pltpu.CompilerParams(
            collective_id=0, has_side_effects=True, vmem_limit_bytes=56 * 2**20
        ),
        cost_estimate=pl.CostEstimate(
            flops=20 * 6 * width**3, bytes_accessed=3 * 2**20, transcendentals=0
        ),
    )(sites, angles, sketch)


def solution(mesh):
    in_specs = (P("chain", "rows", None, None), P("chain", None), P())
    out_specs = P("chain", "rows", None, None)
    return jax.shard_map(
        per_device, mesh=mesh, in_specs=in_specs, out_specs=out_specs, check_vma=False
    )
```

time: 312 us -> 50.7 us (0.16)
  waiting for transfers between devices: 224 us -> 0 us
  Pallas kernels: 0 us -> 48.9 us
  matrix products: 33.4 us -> 0 us
  starting transfers between devices: 20.6 us -> 0 us
  between operations: 18.3 us -> 0.01 us
  other arithmetic: 6.41 us -> 0 us
  local copies, waits for them, and re-layouts: 7.26 us -> 1.67 us
    psum x1 -> x0, waiting for transfers between devices: 76.2 us -> none  [per_device(): gram = lax.psum(jnp.dot(sketched.T, sketched, precision=HIGH), 'rows')]
    reduce_scatter x1 -> x0, waiting for transfers between devices: 60.2 us -> none  [per_device(): lax.psum_scatter(jnp.dot(basis.T, theta, precision=HIGH) / (2.0 * width),...]
    ppermute x8 -> x0, waiting for transfers between devices: 59 us -> none  [from_partner(): return lax.ppermute(block, axis, route)]
    pallas_call x0 -> x1, Pallas kernels: none -> 48.9 us  [per_device(): pl.pallas_call(kernel, out_shape=jax.ShapeDtypeStruct(sites.shape, F32),...]
    dot_general x25 -> x0, matrix products: 33.4 us -> none  [the longest x6 7.38 us: refine(): jnp.dot(own, normed, precision=HIGH)]
    all_gather x1 -> x0, waiting for transfers between devices: 28.9 us -> none  [per_device(): lax.all_gather(right_mat, 'rows', axis=0, tiled=True)]
    ppermute x8 -> x0, starting transfers between devices: 20.5 us -> none  [from_partner(): return lax.ppermute(block, axis, route)]
    dot_general x2 -> x0, local copies, waits for them, and re-layouts: 4.1 us -> none  [the longest x1 4 us: per_device(): jnp.dot(left_mat, lax.all_gather(right_mat, 'rows', axis=0, tiled=True),...]
  transfers between devices with their start and end apart: 11 -> 0, of which waited for: 11 -> 0; matrix products, arithmetic and copies ran while one was open for 1% -> 0% of each run, Pallas kernels for 0% -> 0%
where the time goes in v2:
time: 50.7 us; the launch traced here: 50.6 us
  Pallas kernels  48.9 us (96%)
  local copies, waits for them, and re-layouts  1.67 us (3%)
    pallas_call x1, Pallas kernels, per_device(): pl.pallas_call(kernel, out_shape=jax.ShapeDtypeStruct(sites.shape, F32),...  48.9 us
    unnamed x1, local copies, waits for them, and re-layouts  1.67 us

profile of v2, /device:TPU:1, one launch (start us, length us, event | category | flops | bytes accessed | tf_op | source)
XLA Modules:
  0.0 50.6 jit_solution(294059497840298755)
XLA Ops:
  0.0 48.9 %shard_map.37 = f32[1,64,2,512]{3,2,1,0:T(2,128)} custom-call(f32[1,64,2,512]{3,2,1,0:T(2,128)} %sites.1, f32[1,2]{1,0:T(1,128)} %angles.1, f32[1024,512]{1,0:T(8,128)} %sketch.1), custom_call_target="tpu_custom_call" | custom-call | flops 16106127360 | bytes 3145728 | tf_op jit(solution)/shard_map/pallas_call | solution.py:484
  48.9 1.7 %copy.5 = f32[1,64,2,512]{3,2,1,0:T(2,128)} copy(f32[1,64,2,512]{3,2,1,0:T(2,128)} %shard_map.37) | data formatting | bytes 524288

commit v3 on v2

--- a/solution.py
+++ b/solution.py
@@ -11,11 +11,10 @@
 MESH = pl.DeviceIdType.MESH
 F32 = jnp.float32
 BF16 = jnp.bfloat16
-CUT = 128
 
 RP, RM, FW, B0, BM, BP, BX = range(7)
-G_RWA, G_RWB, G_SA, G_SB, G_R, G_L = range(6)
-Y_RW, Y_SB, Y_ANG, Y_L = range(4)
+G_RW, G_S, G_R, G_L = range(4)
+Y_S, Y_ANG, Y_L = range(3)
 
 
 def split(x):
@@ -42,8 +41,8 @@
 
 def kernel(
     sites, angles, sketch, out,
-    raw, lbuf, rwa, rwb, sa_, sb_, wbuf, wh, wl, zf, xbuf, obuf, ang, trig,
-    ss, rs, vs, vr, loc,
+    raw, lbuf, rw, sbuf, wbuf, wh, wl, zf, xbuf, obuf, ang, trig,
+    ss, rs, vs, vr, loc, ready,
 ):
     chain = lax.axis_index("chain")
     row = lax.axis_index("rows")
@@ -64,8 +63,12 @@
     dev_y = (chain + 1 - 2 * parity, row)
 
     barrier = pltpu.get_barrier_semaphore()
-    for device in (dev_plus, dev_minus, dev_sib, dev_y):
+    for device in (dev_plus, dev_minus, dev_sib):
         pl.semaphore_signal(barrier, inc=1, device_id=device, device_id_type=MESH)
+
+    @pl.when(is_right)
+    def _():
+        pl.semaphore_signal(barrier, inc=1, device_id=dev_y, device_id_type=MESH)
 
     def rows(block):
         return pl.ds(pl.multiple_of(half * block, half), half)
@@ -170,8 +173,7 @@
                 for c in range(self.count):
                     self.sent(kind, c).wait_send()
 
-    ring_rwa, ring_rwb = Ring(rwa, G_RWA, 2), Ring(rwb, G_RWB, 4)
-    ring_sa, ring_sb = Ring(sa_, G_SA, 2), Ring(sb_, G_SB, 4)
+    ring_rw, ring_s = Ring(rw, G_RW, 4), Ring(sbuf, G_S, 4)
     ring_r, ring_l = Ring(raw, G_R, 4), Ring(lbuf, G_L, 4, shared=False)
     chip_l = Ring(lbuf, G_L, 4)
 
@@ -183,8 +185,8 @@
     def l_over_y(n, c):
         return over_y(lbuf, Y_L + n, c, 4, l_blocks[n])
 
-    def ang_copy(site):
-        return remote(ang.at[site], vs.at[Y_ANG, 0], vr.at[Y_ANG, 0], dev_y)
+    def ang_copy():
+        return remote(ang.at[0], vs.at[Y_ANG, 0], vr.at[Y_ANG, 0], dev_y)
 
     def load_sites(view):
         copies = [
@@ -225,102 +227,82 @@
         wl[...] = low
         result = dot3(split(mixed), (wh[...], wl[...]))
         for m in range(2):
-            rwa[m, own, :] = result[half * m : half * (m + 1), :CUT]
-            rwb[m, own, :] = result[half * m : half * (m + 1), CUT:]
-
-    pl.semaphore_wait(barrier, 4)
+            rw[m, own, :] = result[half * m : half * (m + 1)]
+
+    @pl.when(is_left)
+    def _():
+        pl.semaphore_wait(barrier, 4)
+        pl.semaphore_signal(ready, inc=1, device_id=dev_y, device_id_type=MESH)
+
+    @pl.when(is_right)
+    def _():
+        pl.semaphore_wait(barrier, 3)
 
     def all_trig():
-        ang_copy(1 - parity).wait_recv()
+        ang_copy().wait_recv()
         kick, coupling = ang[0, 0:8, :], 0.5 * (ang[0, 8:16, :] + ang[1, 8:16, :])
         trig[0] = jnp.cos(kick)
         trig[1] = jnp.sin(kick)
         trig[2] = jnp.cos(coupling)
         trig[3] = jnp.sin(coupling)
 
-    def rows_of_s(view, into):
+    def rows_of_s():
         ca, sa, cj, sj = (scalar(n) for n in range(4))
         l0, l1 = lbuf[0, own, :], lbuf[1, own, :]
         p, q = ca * l0 - sa * l1, sa * l0 + ca * l1
         lhs = above(beside(cj * p, sj * q), beside(cj * q, -sj * p))
-        result = dot3(split(lhs), split(view[...].reshape(2 * width, view.shape[2])))
+        result = dot3(split(lhs), split(rw[...].reshape(2 * width, width)))
         for s in range(2):
-            into[s, own, :] = result[half * s : half * (s + 1)]
-
-    @pl.when(is_right)
-    def _():
-        ang_copy(parity).start()
-        for c in range(2):
-            over_y(rwa, Y_RW, c, 2).start()
-        ring_rwb.issue()
-        ring_rwb.step1()
-        ring_rwa.issue()
-        ring_rwb.step2()
+            sbuf[s, own, :] = result[half * s : half * (s + 1)]
+
+    @pl.when(is_right)
+    def _():
+        ring_rw.issue()
+        ring_rw.step1()
+        ring_rw.step2()
         all_trig()
         for c in range(4):
             l_over_y(0, c).wait_recv()
-        ring_rwa.step1()
-        ring_rwb.step3()
-        ring_rwb.finish(B0, BM, BP, BX)
-        rows_of_s(rwb, sb_)
+        ring_rw.step3()
+        ring_rw.finish(B0, BM, BP, BX)
+        rows_of_s()
+        pl.semaphore_wait(ready, 1)
         for c in (0, 2, 1, 3):
-            over_y(sb_, Y_SB, c, 4).start()
-        ring_sb.issue()
-        ring_rwa.step2()
-        ring_rwa.step3()
-        ring_rwa.finish(B0, BM, BP, BX)
-        rows_of_s(rwa, sa_)
-        ring_sa.issue()
+            over_y(sbuf, Y_S, c, 4).start()
+        ring_s.issue()
         chip_l.share(B0)
-        ring_sb.step1()
-        ring_sa.step1()
-        ring_sb.step2()
-        ring_sa.step2()
+        ring_s.step1()
+        ring_s.step2()
         ring_r.issue()
 
     @pl.when(is_left)
     def _():
-        ang_copy(parity).start()
+        ang_copy().start()
         for c in range(4):
             l_over_y(0, c).start()
         ring_l.issue()
-        for c in range(2):
-            over_y(rwa, Y_RW, c, 2).wait_recv()
-            ring_rwa.issue_chunk(c)
-        all_trig()
-        ring_rwa.step1()
         ring_l.step1()
         for c in range(2):
             l_over_y(1, c).start()
             l_over_y(2, c + 2).start()
-        ring_rwa.step2()
-        ring_rwa.step3()
-        ring_rwa.finish(B0, BM, BP, BX)
-        rows_of_s(rwa, sa_)
-        ring_sa.issue()
         ring_l.step2()
         for c in range(2):
             l_over_y(1, c + 2).start()
             l_over_y(2, c).start()
-        for c in (0, 2):
-            over_y(sb_, Y_SB, c, 4).wait_recv()
-            ring_sb.issue_chunk(c)
-        ring_sa.step1()
-        for c in (1, 3):
-            over_y(sb_, Y_SB, c, 4).wait_recv()
-            ring_sb.issue_chunk(c)
-        ring_sa.step2()
-        ring_sb.step1()
-        ring_sa.step3()
         ring_l.step3()
         for c in range(4):
             l_over_y(3, c).start()
+        for c in (0, 2, 1, 3):
+            over_y(sbuf, Y_S, c, 4).wait_recv()
+            ring_s.issue_chunk(c)
+        ring_s.step1()
+        ring_s.step2()
 
     cut = width // 2
 
     def add_gram(where, first=False):
         two = pl.ds(pl.multiple_of(2 * half * where, 2 * half), 2 * half)
-        pair = split(above(*(beside(sa_[s, two, :], sb_[s, two, :]) for s in range(2))))
+        pair = split(above(sbuf[0, two, :], sbuf[1, two, :]))
         right = tuple(n[:, cut:] for n in pair)
         top = dot3(tuple(n[:, :cut] for n in pair), pair, ((0,), (0,)))
         low = dot3(right, right, ((0,), (0,)))
@@ -331,34 +313,13 @@
             zf[:cut, :] += top
             zf[cut:, cut:] += low
 
-    def finish_s(*kinds):
-        ring_sa.finish(*kinds)
-        ring_sb.finish(*kinds)
-
-    finish_s(B0)
+    ring_s.finish(B0)
     add_gram(place, first=True)
-
-    @pl.when(is_right)
-    def _():
-        ring_sb.step3()
-
-    @pl.when(is_left)
-    def _():
-        ring_sb.step2()
-
-    finish_s(BM, BP)
+    ring_s.finish(BM, BP)
     add_gram(minus)
     add_gram(plus)
-
-    @pl.when(is_right)
-    def _():
-        ring_sa.step3()
-
-    @pl.when(is_left)
-    def _():
-        ring_sb.step3()
-
-    finish_s(BX)
+    ring_s.step3()
+    ring_s.finish(BX)
     add_gram(across)
     zf[cut:, :cut] = zf[:cut, cut:].T
     gram = zf[...]
@@ -367,7 +328,7 @@
     at_row = lax.broadcasted_iota(jnp.int32, (2 * half, width), 0)
     at_col = lax.broadcasted_iota(jnp.int32, (2 * half, width), 1)
     unit = jnp.where((at_col == at_row + half * row) & (at_row < half), 1.0, 0.0).astype(F32)
-    mine = above(*(beside(sa_[s, own, :], sb_[s, own, :]) for s in range(2)))
+    mine = above(sbuf[0, own, :], sbuf[1, own, :])
     xbuf[...] = jnp.where(is_left, mine, unit)
 
     def refine(step, carry):
@@ -433,7 +394,7 @@
         ca, sa, cj, sj, cb, sb = (scalar(n) for n in range(6))
         cols = split(x[:half] * gain)
         e0, e1 = (
-            dot3(cols, split(beside(sa_[s], sb_[s])), ((1,), (1,))) for s in range(2)
+            dot3(cols, split(sbuf[s]), ((1,), (1,))) for s in range(2)
         )
         f, g = ca * e0 + sa * e1, ca * e1 - sa * e0
         lhs = above(beside(cj * f, cj * g), beside(-sj * g, sj * f))
@@ -452,13 +413,11 @@
     for store in stores:
         store.start()
 
-    ang_copy(parity).wait_send()
-    ring_rwa.drain()
-    ring_sa.drain()
-    ring_sb.drain()
+    ring_s.drain()
 
     @pl.when(is_left)
     def _():
+        ang_copy().wait_send()
         for c in range(4):
             for n in range(4):
                 l_over_y(n, c).wait_send()
@@ -466,11 +425,9 @@
 
     @pl.when(is_right)
     def _():
-        for c in range(2):
-            over_y(rwa, Y_RW, c, 2).wait_send()
         for c in range(4):
-            over_y(sb_, Y_SB, c, 4).wait_send()
-        ring_rwb.drain()
+            over_y(sbuf, Y_S, c, 4).wait_send()
+        ring_rw.drain()
         ring_r.drain()
         chip_l.drain((B0, BM, BP, BX))
 
@@ -493,10 +450,8 @@
         scratch_shapes=[
             vmem((2, width, width), F32),
             vmem((2, width, width), F32),
-            vmem((2, width, CUT), F32),
-            vmem((2, width, width - CUT), F32),
-            vmem((2, width, CUT), F32),
-            vmem((2, width, width - CUT), F32),
+            vmem((2, width, width), F32),
+            vmem((2, width, width), F32),
             vmem((2 * width, width), F32),
             vmem((2 * width, width), BF16),
             vmem((2 * width, width), BF16),
@@ -505,9 +460,9 @@
             vmem((2, half, width), F32),
             vmem((2, 16, 128), F32),
             vmem((6, 8, 128), F32),
-            dma((6, 7, 4)), dma((6, 7, 4)),
-            dma((7, 4)), dma((7, 4)),
-            dma((3,)),
+            dma((4, 7, 4)), dma((4, 7, 4)),
+            dma((6, 4)), dma((6, 4)),
+            dma((3,)), pltpu.SemaphoreType.REGULAR,
         ],
         compiler_params=pltpu.CompilerParams(
             collective_id=0, has_side_effects=True, vmem_limit_bytes=56 * 2**20

time: 50.7 us -> 48.1 us (0.949)
  Pallas kernels: 48.9 us -> 46.3 us
    pallas_call x1, Pallas kernels: 48.9 us -> 46.3 us  [per_device(): pl.pallas_call(kernel, out_shape=jax.ShapeDtypeStruct(sites.shape, F32),...]
where the time goes in v3:
time: 48.1 us; the launch traced here: 47.9 us
  Pallas kernels  46.3 us (96%)
  local copies, waits for them, and re-layouts  1.67 us (3%)
    pallas_call x1, Pallas kernels, per_device(): pl.pallas_call(kernel, out_shape=jax.ShapeDtypeStruct(sites.shape, F32),...  46.3 us
    unnamed x1, local copies, waits for them, and re-layouts  1.67 us

profile of v3, /device:TPU:1, one launch (start us, length us, event | category | flops | bytes accessed | tf_op | source)
XLA Modules:
  0.0 47.9 jit_solution(13937797478647452743)
XLA Ops:
  0.0 46.3 %shard_map.37 = f32[1,64,2,512]{3,2,1,0:T(2,128)} custom-call(f32[1,64,2,512]{3,2,1,0:T(2,128)} %sites.1, f32[1,2]{1,0:T(1,128)} %angles.1, f32[1024,512]{1,0:T(8,128)} %sketch.1), custom_call_target="tpu_custom_call" | custom-call | flops 16106127360 | bytes 3145728 | tf_op jit(solution)/shard_map/pallas_call | solution.py:441
  46.3 1.7 %copy.5 = f32[1,64,2,512]{3,2,1,0:T(2,128)} copy(f32[1,64,2,512]{3,2,1,0:T(2,128)} %shard_map.37) | data formatting | bytes 524288

commit v4 on v3

--- a/solution.py
+++ b/solution.py
@@ -12,6 +12,8 @@
 F32 = jnp.float32
 BF16 = jnp.bfloat16
 
+CHUNKS = 4
+LOW, HIGH = (0, 1), (2, 3)
 RP, RM, FW, B0, BM, BP, BX = range(7)
 G_RW, G_S, G_R, G_L = range(4)
 Y_S, Y_ANG, Y_L = range(3)
@@ -100,93 +102,94 @@
     }
 
     class Ring:
-        def __init__(self, view, which, count, shared=True):
-            self.view, self.which, self.count, self.shared = view, which, count, shared
-            self.low, self.high = range(count // 2), range(count // 2, count)
+        def __init__(self, view, which, shared=True):
+            self.view, self.which, self.shared = view, which, shared
 
         def copy(self, kind, c, block, device):
-            ref = chunk(self.view, block, c, self.count)
-            return remote(ref, ss.at[self.which, kind, c], rs.at[self.which, kind, c], device)
-
-        def sent(self, kind, c):
+            ref = chunk(self.view, block, c, CHUNKS)
+            return remote(ref, ss.at[self.which], rs.at[self.which, kind, c], device)
+
+        def send(self, kind, c):
             if kind == FW:
-                passed = (blk_minus, dev_plus) if c in self.low else (blk_plus, dev_minus)
-                return self.copy(FW, c, *passed)
-            return self.copy(kind, c, *sends[kind])
-
-        def send(self, kind, c):
-            self.sent(kind, c).start()
+                passed = (blk_minus, dev_plus) if c in LOW else (blk_plus, dev_minus)
+                self.copy(FW, c, *passed).start()
+            else:
+                self.copy(kind, c, *sends[kind]).start()
 
         def get(self, kind, c):
             self.copy(kind, c, gets[kind], dev_sib).wait_recv()
 
+        def whole(self, kind, block):
+            ref = self.view.at[:, rows(block)]
+            return remote(ref, ss.at[self.which], rs.at[self.which, kind, 0], dev_sib)
+
+        def share(self, kind):
+            if self.shared:
+                self.whole(kind, sends[kind][0]).start()
+
         def issue(self):
-            for c, d in zip(self.low, self.high):
+            for c, d in zip(LOW, HIGH):
                 self.send(RP, c)
                 self.send(RM, d)
-            for c, d in zip(self.low, self.high):
+            for c, d in zip(LOW, HIGH):
                 self.send(RP, d)
                 self.send(RM, c)
             self.share(B0)
 
-        def share(self, kind):
-            if self.shared:
-                for c in range(self.count):
-                    self.send(kind, c)
-
         def issue_chunk(self, c):
-            for kind in (RP, RM, B0):
-                self.send(kind, c)
+            self.send(RP, c)
+            self.send(RM, c)
 
         def step1(self):
-            for c, d in zip(self.low, self.high):
+            for c, d in zip(LOW, HIGH):
                 self.get(RP, c)
                 self.send(FW, c)
                 self.get(RM, d)
                 self.send(FW, d)
-                if self.shared:
-                    self.send(BM, c)
-                    self.send(BP, d)
 
         def step2(self):
-            for c, d in zip(self.low, self.high):
-                self.get(RP, d)
+            for c in HIGH:
+                self.get(RP, c)
+            self.share(BM)
+            for c in LOW:
                 self.get(RM, c)
-                if self.shared:
-                    self.send(BM, d)
-                    self.send(BP, c)
+            self.share(BP)
 
         def step3(self):
-            for c, d in zip(self.low, self.high):
+            for c, d in zip(LOW, HIGH):
                 for n in (c, d):
                     self.get(FW, n)
                     if self.shared:
-                        self.send(BX, n)
+                        ref = chunk(self.view, blk_across, n, CHUNKS)
+                        remote(ref, ss.at[self.which], rs.at[self.which, BX, 0], dev_sib).start()
 
         def finish(self, *kinds):
             for kind in kinds:
-                for c in range(self.count):
-                    self.get(kind, c)
-
-        def drain(self, kinds=range(7)):
-            for kind in kinds:
-                for c in range(self.count):
-                    self.sent(kind, c).wait_send()
-
-    ring_rw, ring_s = Ring(rw, G_RW, 4), Ring(sbuf, G_S, 4)
-    ring_r, ring_l = Ring(raw, G_R, 4), Ring(lbuf, G_L, 4, shared=False)
-    chip_l = Ring(lbuf, G_L, 4)
+                self.whole(kind, gets[kind]).wait_recv()
+
+        def drain(self, blocks):
+            ref = self.view.at[:, pl.ds(0, half * blocks)]
+            remote(ref, ss.at[self.which], rs.at[self.which, RP, 0], dev_sib).wait_send()
+
+    ring_rw, ring_s = Ring(rw, G_RW), Ring(sbuf, G_S)
+    ring_r, ring_l = Ring(raw, G_R), Ring(lbuf, G_L, shared=False)
+    chip_l = Ring(lbuf, G_L)
 
     def over_y(view, which, c, count, block=row):
-        return remote(chunk(view, block, c, count), vs.at[which, c], vr.at[which, c], dev_y)
+        return remote(chunk(view, block, c, count), vs.at[which], vr.at[which, c], dev_y)
 
     l_blocks = (row, blk_minus, blk_plus, blk_across)
 
     def l_over_y(n, c):
-        return over_y(lbuf, Y_L + n, c, 4, l_blocks[n])
+        ref = chunk(lbuf, l_blocks[n], c, 4)
+        return remote(ref, vs.at[Y_L], vr.at[Y_L + n, c], dev_y)
+
+    def y_drain(view, which, blocks):
+        ref = view.at[:, pl.ds(0, half * blocks)]
+        remote(ref, vs.at[which], vr.at[which, 0], dev_y).wait_send()
 
     def ang_copy():
-        return remote(ang.at[0], vs.at[Y_ANG, 0], vr.at[Y_ANG, 0], dev_y)
+        return remote(ang.at[0], vs.at[Y_ANG], vr.at[Y_ANG, 0], dev_y)
 
     def load_sites(view):
         copies = [
@@ -295,6 +298,7 @@
         for c in (0, 2, 1, 3):
             over_y(sbuf, Y_S, c, 4).wait_recv()
             ring_s.issue_chunk(c)
+        ring_s.share(B0)
         ring_s.step1()
         ring_s.step2()
 
@@ -413,23 +417,20 @@
     for store in stores:
         store.start()
 
-    ring_s.drain()
+    ring_s.drain(7)
 
     @pl.when(is_left)
     def _():
         ang_copy().wait_send()
-        for c in range(4):
-            for n in range(4):
-                l_over_y(n, c).wait_send()
-        ring_l.drain((RP, RM, FW))
-
-    @pl.when(is_right)
-    def _():
-        for c in range(4):
-            over_y(sbuf, Y_S, c, 4).wait_send()
-        ring_rw.drain()
-        ring_r.drain()
-        chip_l.drain((B0, BM, BP, BX))
+        y_drain(lbuf, Y_L, 4)
+        ring_l.drain(3)
+
+    @pl.when(is_right)
+    def _():
+        y_drain(sbuf, Y_S, 1)
+        ring_rw.drain(7)
+        ring_r.drain(7)
+        chip_l.drain(4)
 
     for store in stores:
         store.wait()
@@ -460,8 +461,8 @@
             vmem((2, half, width), F32),
             vmem((2, 16, 128), F32),
             vmem((6, 8, 128), F32),
-            dma((4, 7, 4)), dma((4, 7, 4)),
-            dma((6, 4)), dma((6, 4)),
+            dma((4,)), dma((4, 7, 4)),
+            dma((6,)), dma((6, 4)),
             dma((3,)), pltpu.SemaphoreType.REGULAR,
         ],
         compiler_params=pltpu.CompilerParams(

time: 48.1 us -> 46.9 us (0.975)
  Pallas kernels: 46.3 us -> 45.1 us
    pallas_call x1, Pallas kernels: 46.3 us -> 45.1 us  [per_device(): pl.pallas_call(kernel, out_shape=jax.ShapeDtypeStruct(sites.shape, F32),...]
where the time goes in v4:
time: 46.9 us; the launch traced here: 46.8 us
  Pallas kernels  45.1 us (96%)
  local copies, waits for them, and re-layouts  1.67 us (4%)
    pallas_call x1, Pallas kernels, per_device(): pl.pallas_call(kernel, out_shape=jax.ShapeDtypeStruct(sites.shape, F32),...  45.1 us
    unnamed x1, local copies, waits for them, and re-layouts  1.67 us

profile of v4, /device:TPU:1, one launch (start us, length us, event | category | flops | bytes accessed | tf_op | source)
XLA Modules:
  0.0 46.8 jit_solution(13614786445861873988)
XLA Ops:
  0.0 45.1 %shard_map.37 = f32[1,64,2,512]{3,2,1,0:T(2,128)} custom-call(f32[1,64,2,512]{3,2,1,0:T(2,128)} %sites.1, f32[1,2]{1,0:T(1,128)} %angles.1, f32[1024,512]{1,0:T(8,128)} %sketch.1), custom_call_target="tpu_custom_call" | custom-call | flops 16106127360 | bytes 3145728 | tf_op jit(solution)/shard_map/pallas_call | solution.py:442
  45.1 1.7 %copy.5 = f32[1,64,2,512]{3,2,1,0:T(2,128)} copy(f32[1,64,2,512]{3,2,1,0:T(2,128)} %shard_map.37) | data formatting | bytes 524288

commit v5 on v4

--- a/solution.py
+++ b/solution.py
@@ -323,56 +323,58 @@
     add_gram(minus)
     add_gram(plus)
     ring_s.step3()
-    ring_s.finish(BX)
-    add_gram(across)
-    zf[cut:, :cut] = zf[:cut, cut:].T
-    gram = zf[...]
-    scale = jnp.sqrt(jnp.sum(gram * gram, keepdims=True).reshape(1, 1) + 1e-06)
-    zf[...] = gram / scale
     at_row = lax.broadcasted_iota(jnp.int32, (2 * half, width), 0)
     at_col = lax.broadcasted_iota(jnp.int32, (2 * half, width), 1)
     unit = jnp.where((at_col == at_row + half * row) & (at_row < half), 1.0, 0.0).astype(F32)
     mine = above(sbuf[0, own, :], sbuf[1, own, :])
     xbuf[...] = jnp.where(is_left, mine, unit)
-
-    def refine(step, carry):
+    ring_s.finish(BX)
+    add_gram(across)
+    top, low = zf[:cut, :], zf[cut:, cut:]
+    squares = jnp.sum(top * top) + jnp.sum(low * low) + jnp.sum(top[:, cut:] * top[:, cut:])
+    scale = jnp.sqrt(jnp.full((1, 1), squares, F32) + 1e-06)
+    per = 1.0 / scale
+    zf[:cut, :] = top * per
+    zf[cut:, :cut] = top[:, cut:].T * per
+    zf[cut:, cut:] = low * per
+
+    def refine():
         z, x = zf[...], xbuf[...]
-        z2, x2 = split(z), split(x)
+        z2 = split(z)
         zr = tuple(n[:, cut:] for n in z2)
-        both = dot3(tuple(above(a[:cut], b) for a, b in zip(z2, x2)), z2)
-        top, moved = both[:cut], both[cut:]
+        top = dot3(tuple(n[:cut] for n in z2), z2)
         low = dot3(tuple(n[cut:] for n in z2), zr)
-        xbuf[...] = 1.5 * x - 0.5 * moved
         top2, low2 = split(top), split(low)
         under = tuple(beside(a[:, cut:].T, b) for a, b in zip(top2, low2))
         new_top = 2.25 * z[:cut] - 1.5 * top + 0.25 * dot3(top2, z2)
         new_low = 2.25 * z[cut:, cut:] - 1.5 * low + 0.25 * dot3(under, zr)
+        xbuf[...] = 1.5 * x - 0.5 * dot3(split(x), z2)
         zf[:cut, :] = new_top
         zf[cut:, :cut] = new_top[:, cut:].T
         zf[cut:, cut:] = new_low
 
-        @pl.when(is_right & (step == 0))
-        def _():
-            ring_r.step1()
-            for n, kind in ((1, BM), (2, BP)):
-                for c in range(4):
-                    l_over_y(n, c).wait_recv()
-                chip_l.share(kind)
-
-        @pl.when(is_right & (step == 1))
-        def _():
-            ring_r.step2()
-
-        @pl.when(is_right & (step == ITERS - 3))
-        def _():
-            ring_r.step3()
+    for _ in range((ITERS - 2) // 2):
+        refine()
+
+    @pl.when(is_right)
+    def _():
+        ring_r.step1()
+        for n, kind in ((1, BM), (2, BP)):
             for c in range(4):
-                l_over_y(3, c).wait_recv()
-            chip_l.share(BX)
-
-        return carry
-
-    lax.fori_loop(0, ITERS - 2, refine, 0)
+                l_over_y(n, c).wait_recv()
+            chip_l.share(kind)
+
+    for _ in range((ITERS - 2) // 2):
+        refine()
+
+    @pl.when(is_right)
+    def _():
+        ring_r.step2()
+        for c in range(4):
+            l_over_y(3, c).wait_recv()
+        chip_l.share(BX)
+        ring_r.step3()
+
     z2, x = split(zf[...]), xbuf[...]
 
     def times_z(rows_):

time: 46.9 us -> 46.8 us (level)
  Pallas kernels: 45.1 us -> 44.6 us
    pallas_call x1, Pallas kernels: 45.1 us -> 44.6 us  [per_device(): pl.pallas_call(kernel, out_shape=jax.ShapeDtypeStruct(sites.shape, F32),...]
where the time goes in v5:
time: 46.8 us; the launch traced here: 46.2 us
  Pallas kernels  44.6 us (95%)
  local copies, waits for them, and re-layouts  1.67 us (4%)
    pallas_call x1, Pallas kernels, per_device(): pl.pallas_call(kernel, out_shape=jax.ShapeDtypeStruct(sites.shape, F32),...  44.6 us
    unnamed x1, local copies, waits for them, and re-layouts  1.67 us

profile of v5, /device:TPU:1, one launch (start us, length us, event | category | flops | bytes accessed | tf_op | source)
XLA Modules:
  0.0 46.2 jit_solution(3706847173242805821)
XLA Ops:
  0.0 44.6 %shard_map.37 = f32[1,64,2,512]{3,2,1,0:T(2,128)} custom-call(f32[1,64,2,512]{3,2,1,0:T(2,128)} %sites.1, f32[1,2]{1,0:T(1,128)} %angles.1, f32[1024,512]{1,0:T(8,128)} %sketch.1), custom_call_target="tpu_custom_call" | custom-call | flops 16106127360 | bytes 3145728 | tf_op jit(solution)/shard_map/pallas_call | solution.py:444
  44.6 1.7 %copy.5 = f32[1,64,2,512]{3,2,1,0:T(2,128)} copy(f32[1,64,2,512]{3,2,1,0:T(2,128)} %shard_map.37) | data formatting | bytes 524288

commit v6 on v5

--- a/solution.py
+++ b/solution.py
@@ -39,6 +39,17 @@
 
 def above(*parts):
     return jnp.concatenate(parts, 0)
+
+
+def rows3(a, b, contract=((1,), (0,))):
+    ah, al = a
+    bh, bl = b
+    d = functools.partial(
+        lax.dot_general, dimension_numbers=(contract, ((), ())), preferred_element_type=F32
+    )
+    both = d(above(ah, al), bh)
+    count = ah.shape[0]
+    return both[:count] + (d(ah, bl) + both[count:])
 
 
 def kernel(
@@ -275,8 +286,8 @@
         ring_s.issue()
         chip_l.share(B0)
         ring_s.step1()
+        ring_r.issue()
         ring_s.step2()
-        ring_r.issue()
 
     @pl.when(is_left)
     def _():
@@ -348,7 +359,7 @@
         under = tuple(beside(a[:, cut:].T, b) for a, b in zip(top2, low2))
         new_top = 2.25 * z[:cut] - 1.5 * top + 0.25 * dot3(top2, z2)
         new_low = 2.25 * z[cut:, cut:] - 1.5 * low + 0.25 * dot3(under, zr)
-        xbuf[...] = 1.5 * x - 0.5 * dot3(split(x), z2)
+        xbuf[...] = 1.5 * x - 0.5 * rows3(split(x), z2)
         zf[:cut, :] = new_top
         zf[cut:, :cut] = new_top[:, cut:].T
         zf[cut:, cut:] = new_low
@@ -378,7 +389,7 @@
     z2, x = split(zf[...]), xbuf[...]
 
     def times_z(rows_):
-        return dot3(split(rows_), z2)
+        return rows3(split(rows_), z2)
 
     moved = times_z(x)
     x = 1.5 * x - 0.5 * moved
@@ -400,17 +411,17 @@
         ca, sa, cj, sj, cb, sb = (scalar(n) for n in range(6))
         cols = split(x[:half] * gain)
         e0, e1 = (
-            dot3(cols, split(sbuf[s]), ((1,), (1,))) for s in range(2)
+            rows3(cols, split(sbuf[s]), ((1,), (1,))) for s in range(2)
         )
         f, g = ca * e0 + sa * e1, ca * e1 - sa * e0
         lhs = above(beside(cj * f, cj * g), beside(-sj * g, sj * f))
-        both = dot3(split(lhs), split(lbuf[...].reshape(2 * width, width)))
+        both = rows3(split(lhs), split(lbuf[...].reshape(2 * width, width)))
         c0, c1 = both[:half], both[half:]
         lhs = above(
             beside(cb * c0 - sb * c1, cb * c1 - sb * c0),
             beside(sb * c0 + cb * c1, cb * c0 + sb * c1),
         )
-        right = dot3(split(lhs), split(raw[...].reshape(2 * width, width)))
+        right = rows3(split(lhs), split(raw[...].reshape(2 * width, width)))
         obuf[...] = (right * (1.0 / (2.0 * width))).reshape(2, half, width)
 
     stores = [

time: 46.8 us -> 46.3 us (0.989)
  no operation moved by 1% of the time
where the time goes in v6:
time: 46.3 us; the launch traced here: 46.2 us
  Pallas kernels  44.5 us (96%)
  local copies, waits for them, and re-layouts  1.67 us (4%)
    pallas_call x1, Pallas kernels, per_device(): pl.pallas_call(kernel, out_shape=jax.ShapeDtypeStruct(sites.shape, F32),...  44.5 us
    unnamed x1, local copies, waits for them, and re-layouts  1.67 us

profile of v6, /device:TPU:1, one launch (start us, length us, event | category | flops | bytes accessed | tf_op | source)
XLA Modules:
  0.0 46.2 jit_solution(13231351964880945229)
XLA Ops:
  0.0 44.5 %shard_map.37 = f32[1,64,2,512]{3,2,1,0:T(2,128)} custom-call(f32[1,64,2,512]{3,2,1,0:T(2,128)} %sites.1, f32[1,2]{1,0:T(1,128)} %angles.1, f32[1024,512]{1,0:T(8,128)} %sketch.1), custom_call_target="tpu_custom_call" | custom-call | flops 16106127360 | bytes 3145728 | tf_op jit(solution)/shard_map/pallas_call | solution.py:455
  44.5 1.7 %copy.5 = f32[1,64,2,512]{3,2,1,0:T(2,128)} copy(f32[1,64,2,512]{3,2,1,0:T(2,128)} %shard_map.37) | data formatting | bytes 524288
